TPU v7x, 32 devices: a whole 2x2x4 slice. The times are simulated.
32 devices in a mesh: date: 8 (over y, x, core), row: 4 (over z).
Axes of the slice: x: 2, y: 2, z: 4, core: 2. Of those that a mesh axis runs over, the one named last changes fastest.
Arguments:
- slc: float32 [2, 32, 32, 1024], P(None, 'date', 'row'), may hold values from -6 to 6
- offsets: int32 [2, 32], replicated, may hold values from -2 to 2, as said below
- masks: int32 [5, 32, 1024], P(None, 'row', 'date'), may hold values from 0 to 262143, as said below
Outputs:
- linked: float32 [2, 32, 32, 1024], P(None, None, 'row', 'date')
- eigen: float32 [32, 1024], P('row', 'date')
Inputs may be any that keep to these rules, and one draw needn't show every extreme that they name: `offsets`: row offset in the first row, column offset in the second; some date has 2 in both and another date -2 in both. `masks`: bit (k mod 18) of word k // 18 tells whether slot k of the pixel's neighbourhood is used; the centre slot 40 is always set; bits of slots 81 and above are zero.
All inputs are finite; a program needn't handle non-finite values.
Results may differ from a plain program's by a relative error of at most 0.00011.
Values sent between devices are 32-bit elements; how exact they have to be, the bound alone decides.
No kernel may reach another device: no remote copies, remote signals or barrier semaphores. Data moves between devices by JAX's collectives and lax.ppermute only.
A program may use at most 64 MiB of HBM per device.

v0:
```python
import functools

import jax
import jax.numpy as jnp
from jax import lax
from jax.experimental import pallas as pl
from jax.experimental.pallas import tpu as pltpu
from jax.sharding import PartitionSpec as P

NDATE = 32
SLOT_COLS = 9
EPSILON = 1e-06
LANES = 128
TILE = 8
GROUPS = 8
TAP_COUNT = 8
WINDOW_ROWS = 16
WINDOW_COLS = 136
BLOCKS = 16

FLOAT = jnp.float32
HALF_FLOAT = jnp.bfloat16


def lane_ids(shape):
    return lax.broadcasted_iota(jnp.int32, shape, len(shape) - 1)


def sublane_ids(shape):
    return lax.broadcasted_iota(jnp.int32, shape, len(shape) - 2)


def pack_blocks(slc_ref, send_ref):
    planes = slc_ref.shape[0]
    blocks = send_ref.shape[0]
    for block in range(blocks):
        for plane in range(planes):
            send_ref[block, pl.ds(plane, TILE, stride=planes), :] = slc_ref[
                plane, :, block * LANES : (block + 1) * LANES
            ]
    lanes = lane_ids((planes, LANES))
    rims = [jnp.zeros((planes, LANES), FLOAT) for _ in range(blocks)]
    for row in range(TILE):
        start = 16 * row
        turned = [
            pltpu.roll(
                send_ref[block, row * planes : (row + 1) * planes, :],
                (start + 8) % LANES,
                axis=1,
            )
            for block in range(blocks)
        ]
        left = (lanes >= start) & (lanes < start + 8)
        right = (lanes >= start + 8) & (lanes < start + 16)
        for block in range(blocks):
            if block > 0:
                rims[block] = jnp.where(left, turned[block - 1], rims[block])
            if block < blocks - 1:
                rims[block] = jnp.where(right, turned[block + 1], rims[block])
    for block in range(blocks):
        send_ref[block, TILE * planes : (TILE + 1) * planes, :] = rims[block]


def pack_pieces(slc_ref, *rest):
    pieces, blocks_ref = rest[:-1], rest[-1]
    pack_blocks(slc_ref, blocks_ref)
    here = lax.axis_index("date")
    for turn, piece_ref in enumerate(pieces):
        piece_ref[...] = blocks_ref[here ^ turn]


def join_kernel(turns, *rest):
    here = lax.axis_index("date")
    for turn, piece_ref in zip(turns, rest[:-1]):
        rest[-1][(here ^ turn) % 4] = piece_ref[...]


def tap_weight(distance):
    spread = jnp.abs(2 * distance - 1)
    return jnp.where(spread == 1, 0.5625, jnp.where(spread == 3, -0.0625, 0.0)).astype(FLOAT)


def prepare_kernel(
    offsets_ref, masks_ref, picks_ref, population_ref, row_sub_ref, row_lane_ref, col_lane_ref, words_ref
):
    words = masks_ref.shape[0]
    below = near_is_below()
    total = jnp.zeros((TILE, LANES), jnp.int32)
    for word in range(words):
        bits = masks_ref[word]
        bits = bits - (lax.shift_right_logical(bits, 1) & 0x55555555)
        bits = (bits & 0x33333333) + (lax.shift_right_logical(bits, 2) & 0x33333333)
        bits = (bits + lax.shift_right_logical(bits, 4)) & 0x0F0F0F0F
        bits = bits + lax.shift_right_logical(bits, 8)
        bits = bits + lax.shift_right_logical(bits, 16)
        total = total + (bits & 0xFF)
    population_ref[...] = total.astype(FLOAT)

    lanes = lane_ids((TILE, LANES))
    subs = sublane_ids((TILE, LANES))
    lane_dates = ((lanes % 64) // 8) * 4 + lanes % 4
    row_shift = jnp.zeros((TILE, LANES), jnp.int32)
    col_shift = jnp.zeros((TILE, LANES), jnp.int32)
    for date in range(NDATE):
        here = lane_dates == date
        row_shift = jnp.where(here, offsets_ref[0, date], row_shift)
        col_shift = jnp.where(here, offsets_ref[1, date], col_shift)
    for tap in range(TAP_COUNT):
        row_lane_ref[tap] = tap_weight(tap - 3 - row_shift)
        col_lane_ref[tap] = tap_weight(tap - 3 - col_shift)
    for group in range(GROUPS):
        shift = jnp.zeros((TILE, LANES), jnp.int32)
        for date in range(4):
            shift = jnp.where(subs % 4 == date, offsets_ref[0, 4 * group + date], shift)
        for tap in range(TAP_COUNT):
            row_sub_ref[tap, group * TILE : (group + 1) * TILE, :] = tap_weight(tap - 3 - shift)

    flat = [masks_ref[word] for word in range(words)]
    flat = flat + [jnp.zeros((TILE, LANES), jnp.int32)] * (LANES // TILE - words)
    words_ref[...] = jnp.transpose(jnp.concatenate(flat, axis=0))

    def one_block(block, carry):
        packed = words_ref[pl.ds(pl.multiple_of(block * TILE, TILE), TILE), :]
        for row_pair in range(TILE // 2):
            spread = [[], []]
            for row in (2 * row_pair, 2 * row_pair + 1):
                row_words = [
                    jnp.broadcast_to(
                        packed[:, word * TILE + row : word * TILE + row + 1], (TILE, LANES)
                    )
                    for word in range(words)
                ]
                for half in range(2):
                    near = 8 * half + lanes // 16 - row
                    across = lanes % 16 - subs
                    inside = (near >= 0) & (near <= 8) & (across >= 0) & (across <= 8)
                    amount = jnp.where(inside, (near & 1) * SLOT_COLS + across, 31)
                    first = max(0, 8 * half - row) // 2
                    last = min(8, 8 * half + 7 - row) // 2
                    chosen = row_words[first]
                    for word in range(first + 1, last + 1):
                        chosen = jnp.where(near >= 2 * word, row_words[word], chosen)
                    bits = lax.shift_right_logical(chosen, amount) & 1
                    spread[half].append(bits.astype(FLOAT))
            low_half, high_half = [jnp.concatenate(half, axis=0) for half in spread]
            rows = slice(16 * row_pair, 16 * row_pair + 16)
            picks_ref[block, rows, :LANES] = jnp.where(below, high_half, low_half).astype(HALF_FLOAT)
            picks_ref[block, rows, LANES:] = jnp.where(below, low_half, high_half).astype(HALF_FLOAT)
        return carry

    lax.fori_loop(0, BLOCKS, one_block, 0)


def split_halves(values):
    high = values.astype(HALF_FLOAT)
    low = values - high.astype(FLOAT)
    return high, low


def dot(a, b, contract):
    return lax.dot_general(
        a, b, (((contract[0],), (contract[1],)), ((), ())), preferred_element_type=FLOAT
    )


def packed_rims(base, refs):
    halves = [ref[:, 8 * TILE : 9 * TILE, :].reshape(32, LANES) for ref in refs]
    return jnp.where(
        base == 0, jnp.concatenate(halves, axis=0), jnp.concatenate(halves[::-1], axis=0)
    )


def first_group():
    return (lax.axis_index("date") ^ 4) & 4 if lax.axis_size("date") == GROUPS else 0


def near_is_below():
    return (lax.axis_index("row") + lax.axis_index("date")) % 2 == 0


def resample_rows(
    base,
    own_refs,
    other_refs,
    below,
    row_sub_ref,
    row_lane_ref,
    mixed_ref,
    rims_ref,
    turned_ref,
):
    row_at, row_count = lax.axis_index("row"), lax.axis_size("row")

    exists = (below & (row_at < row_count - 1)) | (jnp.logical_not(below) & (row_at > 0))

    def mix_group(own_ref, other_ref, base, slot):
        group = base + slot
        weights = [
            row_sub_ref[tap, pl.ds(pl.multiple_of(group * TILE, TILE), TILE), :]
            for tap in range(TAP_COUNT)
        ]
        own = [own_ref[slot, row * TILE : (row + 1) * TILE, :] for row in range(TILE)]
        other = [
            jnp.where(exists, other_ref[slot, row * TILE : (row + 1) * TILE, :], 0.0)
            for row in range(TILE)
        ]
        raw = [jnp.where(below, a, b) for a, b in zip(own, other)]
        raw = raw + [jnp.where(below, b, a) for a, b in zip(own, other)]
        for row in range(8):
            mixed = weights[0] * raw[row + 1]
            for tap in range(1, TAP_COUNT):
                mixed = mixed + weights[tap] * raw[row + 1 + tap]
            start = pl.multiple_of((row // 4) * 64 + group * TILE, TILE)
            mixed_ref[row % 4, pl.ds(start, TILE), :] = mixed

    def mix_slot(slot, carry):
        mix_group(own_refs[0], other_refs[0], base, slot)
        mix_group(own_refs[1], other_refs[1], 4 - base, slot)
        return carry

    lax.fori_loop(0, GROUPS // 2, mix_slot, 0)

    lanes = lane_ids((1, LANES))
    lower = lanes < 64
    own, other = [packed_rims(base, refs) for refs in (own_refs, other_refs)]
    other = jnp.where(exists, other, 0.0)
    first, second = jnp.where(below, own, other), jnp.where(below, other, own)
    far_first, far_second = pltpu.roll(first, 64, axis=1), pltpu.roll(second, 64, axis=1)
    rims_ref[0:LANES, :] = jnp.transpose(
        jnp.concatenate([first, jnp.where(lower, far_first, far_second)], axis=0)
    )
    rims_ref[LANES : 2 * LANES, :] = jnp.transpose(jnp.concatenate([second, far_second], axis=0))
    row_weights = [row_lane_ref[tap, 0:1, :] for tap in range(TAP_COUNT)]
    for row in range(4):
        turned_ref[row, 8 : 8 + LANES, :] = jnp.transpose(mixed_ref[row])
        rim = row_weights[0] * rims_ref[(row + 1) * 16 : (row + 2) * 16, :]
        for tap in range(1, TAP_COUNT):
            rim = rim + row_weights[tap] * rims_ref[(row + 1 + tap) * 16 : (row + 2 + tap) * 16, :]
        turned_ref[row, 0:8, :] = rim[0:8]
        turned_ref[row, 8 + LANES : 16 + LANES, :] = rim[8:16]


def resample_columns(below, col_lane_ref, z_ref, y_ref, turned_ref, first, count):
    row_at, row_count = lax.axis_index("row"), lax.axis_size("row")
    col_at, col_count = lax.axis_index("date"), lax.axis_size("date")
    lanes = lane_ids((1, LANES))
    lower = lanes < 64
    width = count * 8 + 8
    places = sublane_ids((width, LANES)) + first * 8
    inside = ((places >= 4) | (col_at > 0)) & ((places < 132) | (col_at < col_count - 1))
    row_inside = (lower & (below | (row_at > 0))) | (
        (lanes >= 64) & (jnp.logical_not(below) | (row_at < row_count - 1))
    )
    inside = inside & row_inside
    term = lax.broadcasted_iota(jnp.int32, (2 * LANES, 2 * LANES), 0) % LANES
    gives = lax.broadcasted_iota(jnp.int32, (2 * LANES, 2 * LANES), 1)
    same_part = ((term % 8) < 4) == (gives < LANES)
    sums = jnp.where(((term < 64) == ((gives % LANES) < 64)) & same_part, 1.0, 0.0).astype(HALF_FLOAT)

    def store_windows(target, row, values):
        high, low = split_halves(values)
        high = high.astype(FLOAT)
        rows = (
            jnp.where(lower, high, pltpu.roll(low, 64, axis=1)),
            jnp.where(lower, pltpu.roll(high, 64, axis=1), low),
        )
        for part in range(2):
            start = (row + 4 * part) * 16
            for block in range(count):
                target[first + block, start : start + 16, :] = rows[part][
                    block * 8 : block * 8 + 16
                ].astype(HALF_FLOAT)

    for row in range(4):
        begin = 1 + first * 8
        mixed = col_lane_ref[0, 0:1, :] * turned_ref[row, begin : begin + width, :]
        for tap in range(1, TAP_COUNT):
            mixed = mixed + col_lane_ref[tap, 0:1, :] * turned_ref[
                row, begin + tap : begin + tap + width, :
            ]
        z = jnp.where(inside, mixed, 0.0)
        high, low = split_halves(z)
        total = dot(jnp.concatenate([high, low.astype(HALF_FLOAT)], axis=1), sums, (1, 0))
        y = z * total[:, :LANES] + swapped(z) * total[:, LANES:]
        store_windows(z_ref, row, z)
        store_windows(y_ref, row, y)


def swapped(values):
    real = (lane_ids((1, LANES)) % 8) < 4
    return jnp.where(real, pltpu.roll(values, LANES - 4, axis=1), -pltpu.roll(values, 4, axis=1))


def near_kernel(
    own_b,
    own_a,
    near_b,
    near_a,
    row_sub_ref,
    row_lane_ref,
    col_lane_ref,
    z_ref,
    y_ref,
    mixed_ref,
    rims_ref,
    turned_ref,
):
    below = near_is_below()
    resample_rows(
        first_group(),
        (own_a, own_b),
        (near_a, near_b),
        below,
        row_sub_ref,
        row_lane_ref,
        mixed_ref,
        rims_ref,
        turned_ref,
    )
    resample_columns(below, col_lane_ref, z_ref, y_ref, turned_ref, 0, BLOCKS)


def link_kernel(
    own_b,
    own_a,
    far_b,
    far_a,
    row_sub_ref,
    row_lane_ref,
    col_lane_ref,
    near_z_ref,
    near_y_ref,
    picks_ref,
    population_ref,
    linked_ref,
    eigen_ref,
    far_z_ref,
    far_y_ref,
    mixed_ref,
    rims_ref,
    turned_ref,
    result_ref,
    first_ref,
    vectors_ref,
    chosen_ref,
):
    below = jnp.logical_not(near_is_below())
    resample_rows(
        first_group(),
        (own_a, own_b),
        (far_a, far_b),
        below,
        row_sub_ref,
        row_lane_ref,
        mixed_ref,
        rims_ref,
        turned_ref,
    )
    lower = lane_ids((1, LANES)) < 64

    def columns(first, count):
        resample_columns(below, col_lane_ref, far_z_ref, far_y_ref, turned_ref, first, count)

    def first_phase(first, count):
        for block in range(first, first + count):
            y = jnp.concatenate([near_y_ref[block], far_y_ref[block]], axis=0)
            vector = dot(picks_ref[block], y, (1, 0))
            vector = vector + pltpu.roll(vector, 64, axis=1)
            high, low = split_halves(jnp.concatenate([vector, swapped(vector)], axis=0))
            first_ref[block] = vector
            vectors_ref[block, :, :LANES] = high
            vectors_ref[block, :, LANES:] = low.astype(HALF_FLOAT)

    def inner_phase(first, count):
        for block in range(first, first + count):
            z = jnp.concatenate([near_z_ref[block], far_z_ref[block]], axis=0)
            inner = dot(vectors_ref[block], jnp.concatenate([z, z], axis=1), (1, 1))
            high, low = split_halves(inner)
            picks = picks_ref[block]
            picks = jnp.concatenate([picks, picks], axis=0)
            chosen_ref[block, :128, :] = high * picks
            chosen_ref[block, 128:, :] = low.astype(HALF_FLOAT) * picks

    def outer_phase(first, count):
        for block in range(first, first + count):
            z = jnp.concatenate([near_z_ref[block], far_z_ref[block]], axis=0)
            outer = dot(chosen_ref[block], z, (1, 0))
            outer = outer[:128] + outer[128:]
            outer = outer + pltpu.roll(outer, 64, axis=1)
            second = outer[:64] - swapped(outer[64:])
            both = jnp.where(lower, second, first_ref[block])
            for row in range(8):
                result_ref[row, block * 8 : block * 8 + 8, :] = both[row * 8 : row * 8 + 8]

    half = BLOCKS // 2
    columns(0, half)
    first_phase(0, half)
    columns(half, half)
    inner_phase(0, half)
    first_phase(half, half)
    outer_phase(0, half)
    inner_phase(half, half)
    outer_phase(half, half)

    inverse = 1.0 / population_ref[...]
    for row in range(8):
        turned = jnp.transpose(result_ref[row])
        second, first = turned[:64], turned[64:]
        scale = inverse[row : row + 1]
        square = scale * scale
        norm_first = jnp.sqrt(jnp.sum(first * first, axis=0, keepdims=True) * square + EPSILON)
        norm_last = jnp.sqrt(
            jnp.sum(second * second, axis=0, keepdims=True) * (square * square) + EPSILON
        )
        eigen_ref[row : row + 1, :] = norm_last / norm_first
        linked = second * (square * (jnp.sqrt(jnp.float32(NDATE)) / norm_last))
        for group in range(GROUPS):
            for part in range(2):
                begin = ((part * NDATE + 4 * group) * 8) + row
                at = group * 8 + part * 4
                linked_ref[pl.ds(begin, 4, stride=8), :] = linked[at : at + 4]


def canonical(received, dates_dev):
    sources = received.shape[0]
    if dates_dev == 4:
        return received
    cells = received.reshape(sources, 9, 2, dates_dev, LANES)
    cells = jnp.transpose(cells, (1, 2, 0, 3, 4)).reshape(9, 2, GROUPS, 4, LANES)
    return jnp.transpose(cells, (2, 0, 1, 3, 4)).reshape(GROUPS, 9 * TILE, LANES)


def partner(date, row, turn, rows_count):
    other = row + 1 if (row + date + turn) % 2 == 0 else row - 1
    if 0 <= other < rows_count:
        return date * rows_count + other
    return (date ^ 2) * rows_count + row


def vmem(count):
    return [pl.BlockSpec(memory_space=pltpu.VMEM)] * count


def on_device(slc, offsets, masks):
    dates_dev = slc.shape[1]
    rows_dev = slc.shape[2]
    cols_all = slc.shape[3]
    rows_count = lax.axis_size("row")
    cols_count = lax.axis_size("date")
    planes_dev = 2 * dates_dev
    assert rows_dev == TILE and cols_all == cols_count * LANES

    small = pltpu.CompilerParams(vmem_limit_bytes=4 * 1024 * 1024)
    images = slc.reshape(planes_dev, rows_dev, cols_all)
    moves = pl.CostEstimate(flops=0, bytes_accessed=600_000, transcendentals=0)
    half_shape = jax.ShapeDtypeStruct((GROUPS // 2, 9 * TILE, LANES), FLOAT)

    def swap_rows(cells, turn):
        return lax.ppermute(
            cells,
            ("date", "row"),
            [
                (date * rows_count + row, partner(date, row, turn, rows_count))
                for date in range(cols_count)
                for row in range(rows_count)
            ],
        )

    if cols_count == GROUPS:
        pieces = pl.pallas_call(
            pack_pieces,
            out_shape=[jax.ShapeDtypeStruct((9 * TILE, LANES), FLOAT)] * GROUPS,
            in_specs=vmem(1),
            out_specs=vmem(GROUPS),
            scratch_shapes=[pltpu.VMEM((GROUPS, 9 * TILE, LANES), FLOAT)],
            compiler_params=small,
            cost_estimate=moves,
            name="pack",
        )(images)
        pieces = list(pieces[:1]) + [
            lax.ppermute(pieces[turn], "date", [(i, i ^ turn) for i in range(GROUPS)])
            for turn in range(1, GROUPS)
        ]
        own = [
            pl.pallas_call(
                functools.partial(join_kernel, turns),
                out_shape=half_shape,
                in_specs=vmem(4),
                out_specs=vmem(1)[0],
                compiler_params=small,
                cost_estimate=moves,
                name="join",
            )(*[pieces[turn] for turn in turns])
            for turns in ((6, 7, 4, 5), (2, 3, 1, 0))
        ]
    else:
        outgoing = pl.pallas_call(
            pack_blocks,
            out_shape=jax.ShapeDtypeStruct((cols_count, 9 * planes_dev, LANES), FLOAT),
            in_specs=vmem(1),
            out_specs=vmem(1)[0],
            compiler_params=small,
            cost_estimate=moves,
            name="pack",
        )(images)
        received = lax.all_to_all(outgoing, "date", split_axis=0, concat_axis=0, tiled=True)
        received = canonical(received, dates_dev)
        own = [received[: GROUPS // 2], received[GROUPS // 2 :]]
    near_a, far_a, near_b, far_b = [swap_rows(half, turn) for half in own for turn in range(2)]

    picks, population, row_sub, row_lane, col_lane = pl.pallas_call(
        prepare_kernel,
        out_shape=(
            jax.ShapeDtypeStruct((BLOCKS, 64, 256), HALF_FLOAT),
            jax.ShapeDtypeStruct((TILE, LANES), FLOAT),
            jax.ShapeDtypeStruct((TAP_COUNT, 64, LANES), FLOAT),
            jax.ShapeDtypeStruct((TAP_COUNT, TILE, LANES), FLOAT),
            jax.ShapeDtypeStruct((TAP_COUNT, TILE, LANES), FLOAT),
        ),
        in_specs=[pl.BlockSpec(memory_space=pltpu.SMEM)] + vmem(1),
        out_specs=tuple(vmem(5)),
        scratch_shapes=[pltpu.VMEM((LANES, LANES), jnp.int32)],
        compiler_params=small,
        cost_estimate=pl.CostEstimate(flops=4_000_000, bytes_accessed=1_000_000, transcendentals=0),
        name="prepare",
    )(offsets, masks)

    half_scratch = [
        pltpu.VMEM((4, LANES, LANES), FLOAT),
        pltpu.VMEM((2 * LANES, LANES), FLOAT),
        pltpu.VMEM((4, LANES + 16, LANES), FLOAT),
    ]
    windows = jax.ShapeDtypeStruct((BLOCKS, LANES, LANES), HALF_FLOAT)
    near_z, near_y = pl.pallas_call(
        near_kernel,
        out_shape=(windows, windows),
        in_specs=vmem(7),
        out_specs=tuple(vmem(2)),
        scratch_shapes=half_scratch,
        compiler_params=small,
        cost_estimate=pl.CostEstimate(
            flops=200_000_000, bytes_accessed=2_000_000, transcendentals=0
        ),
        name="near",
    )(*own[::-1], near_b, near_a, row_sub, row_lane, col_lane)
    linked, eigen = pl.pallas_call(
        link_kernel,
        out_shape=(
            jax.ShapeDtypeStruct((2 * NDATE * TILE, LANES), FLOAT),
            jax.ShapeDtypeStruct((TILE, LANES), FLOAT),
        ),
        in_specs=vmem(11),
        out_specs=tuple(vmem(2)),
        scratch_shapes=[
            pltpu.VMEM((BLOCKS, LANES, LANES), HALF_FLOAT),
            pltpu.VMEM((BLOCKS, LANES, LANES), HALF_FLOAT),
        ]
        + half_scratch
        + [
            pltpu.VMEM((8, LANES, LANES), FLOAT),
            pltpu.VMEM((BLOCKS, 64, LANES), FLOAT),
            pltpu.VMEM((BLOCKS, 128, 256), HALF_FLOAT),
            pltpu.VMEM((BLOCKS, 256, 256), HALF_FLOAT),
        ],
        compiler_params=pltpu.CompilerParams(vmem_limit_bytes=16 * 1024 * 1024),
        cost_estimate=pl.CostEstimate(
            flops=1_000_000_000, bytes_accessed=2_000_000, transcendentals=0
        ),
        name="link",
    )(*own[::-1], far_b, far_a, row_sub, row_lane, col_lane, near_z, near_y, picks, population)
    return linked.reshape(2, NDATE, TILE, LANES), eigen


def solution(mesh):
    in_specs = (P(None, "date", "row", None), P(), P(None, "row", "date"))
    out_specs = (P(None, None, "row", "date"), P("row", "date"))
    return jax.shard_map(
        on_device, mesh=mesh, in_specs=in_specs, out_specs=out_specs, check_vma=False
    )
```

profile of v0, /device:TPU:0, one launch (start us, length us, event | category | flops | bytes accessed | tf_op | source)
XLA Modules:
  0.0 24.7 jit_solution(3384429699387969245)
XLA Ops:
  0.6 0.0 copy-start
  0.6 0.9 %copy-done = f32[2,4,8,1024]{3,2,1,0:T(8,128)S(1)} copy-done((f32[2,4,8,1024]{3,2,1,0:T(8,128)S(1)}, f32[2,4,8,1024]{3,2,1,0:T(8,128)}, u32[]{:S(2)}) %copy-start) | copy-done | bytes 262168
  1.6 0.2 pack.1
  1.8 4.0 %collective-permute-start.3 = (f32[72,128]{1,0:T(8,128)S(1)}, f32[72,128]{1,0:T(8,128)S(1)}, u32[]{:S(2)}, u32[]{:S(2)}) collective-permute-start(f32[72,128]{1,0:T(8,128)S(1)} %get-tuple-element.23), channel_id=1, source_target_pairs={{0,24},{4,28},{8,16},{12,20},{16,8},{20,12},{24,0},{28,4},{1,25},{... | collective-permute-start | bytes 110600 | tf_op jit(solution)/shard_map/ppermute | solution.py:481
  5.7 0.0 collective-permute-start.4
  5.7 1.2 %collective-permute-start.5 = (f32[72,128]{1,0:T(8,128)S(1)}, f32[72,128]{1,0:T(8,128)S(1)}, u32[]{:S(2)}, u32[]{:S(2)}) collective-permute-start(f32[72,128]{1,0:T(8,128)S(1)} %get-tuple-element.25), channel_id=1, source_target_pairs={{0,16},{4,20},{8,24},{12,28},{16,0},{20,4},{24,8},{28,12},{1,17},{... | collective-permute-start | bytes 110600 | tf_op jit(solution)/shard_map/ppermute | solution.py:481
  6.9 0.6 %collective-permute-start.6 = (f32[72,128]{1,0:T(8,128)S(1)}, f32[72,128]{1,0:T(8,128)S(1)}, u32[]{:S(2)}, u32[]{:S(2)}) collective-permute-start(f32[72,128]{1,0:T(8,128)S(1)} %get-tuple-element.26), channel_id=1, source_target_pairs={{0,20},{4,16},{8,28},{12,24},{16,4},{20,0},{24,12},{28,8},{1,21},{... | collective-permute-start | bytes 110600 | tf_op jit(solution)/shard_map/ppermute | solution.py:481
  7.5 1.7 %collective-permute-start = (f32[72,128]{1,0:T(8,128)S(1)}, f32[72,128]{1,0:T(8,128)S(1)}, u32[]{:S(2)}, u32[]{:S(2)}) collective-permute-start(f32[72,128]{1,0:T(8,128)S(1)} %get-tuple-element.19), channel_id=1, source_target_pairs={{0,8},{4,12},{8,0},{12,4},{16,24},{20,28},{24,16},{28,20},{1,9},{5... | collective-permute-start | bytes 110600 | tf_op jit(solution)/shard_map/ppermute | solution.py:481
  9.2 0.0 collective-permute-done.3.rest_0_
  9.2 0.1 collective-permute-start.1
  9.2 1.0 %collective-permute-done.4.rest_1_ = f32[72,128]{1,0:T(8,128)S(1)} collective-permute-done((f32[72,128]{1,0:T(8,128)S(1)}, f32[72,128]{1,0:T(8,128)S(1)}, u32[]{:S(2)}, u32[]{:S(2)}) %collective-permute-start.4) | collective-permute-done | bytes 36896 | tf_op jit(solution)/shard_map/ppermute | solution.py:481
  10.3 0.0 collective-permute-start.2
  10.3 0.5 %collective-permute-done.5.rest_2_ = f32[72,128]{1,0:T(8,128)S(1)} collective-permute-done((f32[72,128]{1,0:T(8,128)S(1)}, f32[72,128]{1,0:T(8,128)S(1)}, u32[]{:S(2)}, u32[]{:S(2)}) %collective-permute-start.5) | collective-permute-done | bytes 36896 | tf_op jit(solution)/shard_map/ppermute | solution.py:481
  10.7 0.3 %collective-permute-done.6.rest_3_ = f32[72,128]{1,0:T(8,128)S(1)} collective-permute-done((f32[72,128]{1,0:T(8,128)S(1)}, f32[72,128]{1,0:T(8,128)S(1)}, u32[]{:S(2)}, u32[]{:S(2)}) %collective-permute-start.6) | collective-permute-done | bytes 36896 | tf_op jit(solution)/shard_map/ppermute | solution.py:481
  11.1 1.7 %collective-permute-start.10 = (f32[4,72,128]{2,1,0:T(8,128)S(1)}, f32[4,72,128]{2,1,0:T(8,128)S(1)}, u32[]{:S(2)}, u32[]{:S(2)}) collective-permute-start(f32[4,72,128]{2,1,0:T(8,128)S(1)} %join.3.own_a), channel_id=1, source_target_pairs={{0,1},{1,0},{2,3},{3,2},{4,12},{5,6},{6,5},{7,15},{8,9},{9,8},{10,... | collective-permute-start | bytes 442376 | tf_op jit(solution)/shard_map/ppermute | solution.py:459
  12.7 0.0 collective-permute-done.rest_0_
  12.7 0.0 collective-permute-done.1.rest_1_
  12.8 0.0 collective-permute-done.2.rest_2_
  12.8 0.0 copy-start.1
  12.8 0.0 copy-start.2
  12.8 1.6 %collective-permute-start.9 = (f32[4,72,128]{2,1,0:T(8,128)S(1)}, f32[4,72,128]{2,1,0:T(8,128)S(1)}, u32[]{:S(2)}, u32[]{:S(2)}) collective-permute-start(f32[4,72,128]{2,1,0:T(8,128)S(1)} %join.2.own_b), channel_id=1, source_target_pairs={{0,1},{1,0},{2,3},{3,2},{4,12},{5,6},{6,5},{7,15},{8,9},{9,8},{10,... | collective-permute-start | bytes 442376 | tf_op jit(solution)/shard_map/ppermute | solution.py:459
  14.4 0.8 %collective-permute-start.8 = (f32[4,72,128]{2,1,0:T(8,128)S(1)}, f32[4,72,128]{2,1,0:T(8,128)S(1)}, u32[]{:S(2)}, u32[]{:S(2)}) collective-permute-start(f32[4,72,128]{2,1,0:T(8,128)S(1)} %join.3.own_a), channel_id=1, source_target_pairs={{0,8},{1,2},{2,1},{3,11},{4,5},{5,4},{6,7},{7,6},{8,0},{9,10},{10,... | collective-permute-start | bytes 442376 | tf_op jit(solution)/shard_map/ppermute | solution.py:459
  15.2 1.3 %collective-permute-start.7 = (f32[4,72,128]{2,1,0:T(8,128)S(1)}, f32[4,72,128]{2,1,0:T(8,128)S(1)}, u32[]{:S(2)}, u32[]{:S(2)}) collective-permute-start(f32[4,72,128]{2,1,0:T(8,128)S(1)} %join.2.own_b), channel_id=1, source_target_pairs={{0,8},{1,2},{2,1},{3,11},{4,5},{5,4},{6,7},{7,6},{8,0},{9,10},{10,... | collective-permute-start | bytes 442376 | tf_op jit(solution)/shard_map/ppermute | solution.py:459
  16.5 0.0 copy-done.1
  16.5 0.0 copy-done.2
  16.5 2.9 %prepare.1 = (bf16[16,64,256]{2,1,0:T(8,128)(2,1)S(1)}, f32[8,128]{1,0:T(8,128)S(1)}, f32[8,64,128]{2,1,0:T(8,128)S(1)}, f32[8,8,128]{2,1,0:T(8,128)S(1)}, f32[8,8,128]{2,1,0:T(8,128)S(1)}) custom-call(s32[2,32]{1,0:T(2,128)S(1)} %copy-done.2, s32[5,8,128]{2,1,0:T(8,128)S(1)} %copy-done.1), custom_call_target="tpu_custom_call" | custom-call | flops 4000000 | bytes 1000000 | tf_op jit(solution)/shard_map/prepare/pallas_call | solution.py:511
  19.4 0.0 collective-permute-done.10.near_a
  19.4 0.1 collective-permute-done.9.near_b
  19.5 0.9 %near.1 = (bf16[16,128,128]{2,1,0:T(8,128)(2,1)S(1)}, bf16[16,128,128]{2,1,0:T(8,128)(2,1)S(1)}) custom-call(f32[4,72,128]{2,1,0:T(8,128)S(1)} %join.2.own_b, f32[4,72,128]{2,1,0:T(8,128)S(1)} %join.3.own_a, f32[4,72,128]{2,1,0:T(8,128)S(1)} %collective-permute-done.9.near_b, f32[4,72,128]{2,1,0:T(8,128)S(1)} %collective-permute-done.10.near_a, ...), custom_call_target="tpu_custom_call" | custom-call | flops 200000000 | bytes 2000000 | tf_op jit(solution)/shard_map/near/pallas_call | solution.py:534
  20.5 0.0 collective-permute-done.8.far_a
  20.5 0.7 %collective-permute-done.7.far_b = f32[4,72,128]{2,1,0:T(8,128)S(1)} collective-permute-done((f32[4,72,128]{2,1,0:T(8,128)S(1)}, f32[4,72,128]{2,1,0:T(8,128)S(1)}, u32[]{:S(2)}, u32[]{:S(2)}) %collective-permute-start.7) | collective-permute-done | bytes 147488 | tf_op jit(solution)/shard_map/ppermute | solution.py:459
  21.2 3.5 %link.1 = (f32[512,128]{1,0:T(8,128)}, f32[8,128]{1,0:T(8,128)}) custom-call(f32[4,72,128]{2,1,0:T(8,128)S(1)} %join.2.own_b, f32[4,72,128]{2,1,0:T(8,128)S(1)} %join.3.own_a, f32[4,72,128]{2,1,0:T(8,128)S(1)} %collective-permute-done.7.far_b, f32[4,72,128]{2,1,0:T(8,128)S(1)} %collective-permute-done.8.far_a, ...), custom_call_target="tpu_custom_call" | custom-call | flops 1000000000 | bytes 2000000 | tf_op jit(solution)/shard_map/link/pallas_call | solution.py:546
  (2 shorter events, 0.0 us)
Async XLA Ops:
  0.6 1.0 %copy-start = (f32[2,4,8,1024]{3,2,1,0:T(8,128)S(1)}, f32[2,4,8,1024]{3,2,1,0:T(8,128)}, u32[]{:S(2)}) copy-start(f32[2,4,8,1024]{3,2,1,0:T(8,128)} %param.3) | copy-start | bytes 786436
  1.8 7.4 %collective-permute-start.3 = (f32[72,128]{1,0:T(8,128)S(1)}, f32[72,128]{1,0:T(8,128)S(1)}, u32[]{:S(2)}, u32[]{:S(2)}) collective-permute-start(f32[72,128]{1,0:T(8,128)S(1)} %get-tuple-element.23), channel_id=1, source_target_pairs={{0,24},{4,28},{8,16},{12,20},{16,8},{20,12},{24,0},{28,4},{1,25},{... | collective-permute-start | bytes 110600 | tf_op jit(solution)/shard_map/ppermute | solution.py:481
  5.7 4.5 %collective-permute-start.4 = (f32[72,128]{1,0:T(8,128)S(1)}, f32[72,128]{1,0:T(8,128)S(1)}, u32[]{:S(2)}, u32[]{:S(2)}) collective-permute-start(f32[72,128]{1,0:T(8,128)S(1)} %get-tuple-element.24), channel_id=1, source_target_pairs={{0,28},{4,24},{8,20},{12,16},{16,12},{20,8},{24,4},{28,0},{1,29},{... | collective-permute-start | bytes 110600 | tf_op jit(solution)/shard_map/ppermute | solution.py:481
  5.7 5.0 %collective-permute-start.5 = (f32[72,128]{1,0:T(8,128)S(1)}, f32[72,128]{1,0:T(8,128)S(1)}, u32[]{:S(2)}, u32[]{:S(2)}) collective-permute-start(f32[72,128]{1,0:T(8,128)S(1)} %get-tuple-element.25), channel_id=1, source_target_pairs={{0,16},{4,20},{8,24},{12,28},{16,0},{20,4},{24,8},{28,12},{1,17},{... | collective-permute-start | bytes 110600 | tf_op jit(solution)/shard_map/ppermute | solution.py:481
  6.9 4.1 %collective-permute-start.6 = (f32[72,128]{1,0:T(8,128)S(1)}, f32[72,128]{1,0:T(8,128)S(1)}, u32[]{:S(2)}, u32[]{:S(2)}) collective-permute-start(f32[72,128]{1,0:T(8,128)S(1)} %get-tuple-element.26), channel_id=1, source_target_pairs={{0,20},{4,16},{8,28},{12,24},{16,4},{20,0},{24,12},{28,8},{1,21},{... | collective-permute-start | bytes 110600 | tf_op jit(solution)/shard_map/ppermute | solution.py:481
  7.5 5.2 %collective-permute-start = (f32[72,128]{1,0:T(8,128)S(1)}, f32[72,128]{1,0:T(8,128)S(1)}, u32[]{:S(2)}, u32[]{:S(2)}) collective-permute-start(f32[72,128]{1,0:T(8,128)S(1)} %get-tuple-element.19), channel_id=1, source_target_pairs={{0,8},{4,12},{8,0},{12,4},{16,24},{20,28},{24,16},{28,20},{1,9},{5... | collective-permute-start | bytes 110600 | tf_op jit(solution)/shard_map/ppermute | solution.py:481
  9.2 3.6 %collective-permute-start.1 = (f32[72,128]{1,0:T(8,128)S(1)}, f32[72,128]{1,0:T(8,128)S(1)}, u32[]{:S(2)}, u32[]{:S(2)}) collective-permute-start(f32[72,128]{1,0:T(8,128)S(1)} %get-tuple-element.20), channel_id=1, source_target_pairs={{0,12},{4,8},{8,4},{12,0},{16,28},{20,24},{24,20},{28,16},{1,13},{... | collective-permute-start | bytes 110600 | tf_op jit(solution)/shard_map/ppermute | solution.py:481
  10.3 2.5 %collective-permute-start.2 = (f32[72,128]{1,0:T(8,128)S(1)}, f32[72,128]{1,0:T(8,128)S(1)}, u32[]{:S(2)}, u32[]{:S(2)}) collective-permute-start(f32[72,128]{1,0:T(8,128)S(1)} %get-tuple-element.21), channel_id=1, source_target_pairs={{0,4},{4,0},{8,12},{12,8},{16,20},{20,16},{24,28},{28,24},{1,5},{5... | collective-permute-start | bytes 110600 | tf_op jit(solution)/shard_map/ppermute | solution.py:481
  11.1 8.3 %collective-permute-start.10 = (f32[4,72,128]{2,1,0:T(8,128)S(1)}, f32[4,72,128]{2,1,0:T(8,128)S(1)}, u32[]{:S(2)}, u32[]{:S(2)}) collective-permute-start(f32[4,72,128]{2,1,0:T(8,128)S(1)} %join.3.own_a), channel_id=1, source_target_pairs={{0,1},{1,0},{2,3},{3,2},{4,12},{5,6},{6,5},{7,15},{8,9},{9,8},{10,... | collective-permute-start | bytes 442376 | tf_op jit(solution)/shard_map/ppermute | solution.py:459
  12.8 3.7 %copy-start.1 = (s32[5,8,128]{2,1,0:T(8,128)S(1)}, s32[5,8,128]{2,1,0:T(8,128)}, u32[]{:S(2)}) copy-start(s32[5,8,128]{2,1,0:T(8,128)} %masks_ref.1) | copy-start | bytes 61444
  12.8 3.7 %copy-start.2 = (s32[2,32]{1,0:T(2,128)S(1)}, s32[2,32]{1,0:T(2,128)}, u32[]{:S(2)}) copy-start(s32[2,32]{1,0:T(2,128)} %offsets_ref.1) | copy-start | bytes 772
  12.8 6.7 %collective-permute-start.9 = (f32[4,72,128]{2,1,0:T(8,128)S(1)}, f32[4,72,128]{2,1,0:T(8,128)S(1)}, u32[]{:S(2)}, u32[]{:S(2)}) collective-permute-start(f32[4,72,128]{2,1,0:T(8,128)S(1)} %join.2.own_b), channel_id=1, source_target_pairs={{0,1},{1,0},{2,3},{3,2},{4,12},{5,6},{6,5},{7,15},{8,9},{9,8},{10,... | collective-permute-start | bytes 442376 | tf_op jit(solution)/shard_map/ppermute | solution.py:459
  14.4 6.0 %collective-permute-start.8 = (f32[4,72,128]{2,1,0:T(8,128)S(1)}, f32[4,72,128]{2,1,0:T(8,128)S(1)}, u32[]{:S(2)}, u32[]{:S(2)}) collective-permute-start(f32[4,72,128]{2,1,0:T(8,128)S(1)} %join.3.own_a), channel_id=1, source_target_pairs={{0,8},{1,2},{2,1},{3,11},{4,5},{5,4},{6,7},{7,6},{8,0},{9,10},{10,... | collective-permute-start | bytes 442376 | tf_op jit(solution)/shard_map/ppermute | solution.py:459
  15.2 6.0 %collective-permute-start.7 = (f32[4,72,128]{2,1,0:T(8,128)S(1)}, f32[4,72,128]{2,1,0:T(8,128)S(1)}, u32[]{:S(2)}, u32[]{:S(2)}) collective-permute-start(f32[4,72,128]{2,1,0:T(8,128)S(1)} %join.2.own_b), channel_id=1, source_target_pairs={{0,8},{1,2},{2,1},{3,11},{4,5},{5,4},{6,7},{7,6},{8,0},{9,10},{10,... | collective-permute-start | bytes 442376 | tf_op jit(solution)/shard_map/ppermute | solution.py:459
where the time goes:
time: 24.8 us; the launch traced here: 24.7 us
  starting transfers between devices  12.8 us (52%)
  Pallas kernels  7.6 us (31%)
  waiting for transfers between devices  2.63 us (11%)
  local copies, waits for them, and re-layouts  0.95 us (4%)
  between operations  0.7 us (3%)
    ppermute x7, starting transfers between devices, on_device(): lax.ppermute(pieces[turn], 'date', [(i, i ^ turn) for i in range(GROUPS)])  7.46 us
    ppermute x4, starting transfers between devices, swap_rows(): lax.ppermute(cells, ('date', 'row'), [(date * rows_count + row, partner(d...  5.32 us
    pallas_call x1, Pallas kernels, on_device(): pl.pallas_call(link_kernel, out_shape=(jax.ShapeDtypeStruct((2 * NDATE *...  3.5 us
    pallas_call x1, Pallas kernels, on_device(): pl.pallas_call(prepare_kernel, out_shape=(jax.ShapeDtypeStruct((BLOCKS, 6...  2.92 us
    ppermute x7, waiting for transfers between devices, on_device(): lax.ppermute(pieces[turn], 'date', [(i, i ^ turn) for i in range(GROUPS)])  1.83 us
    unnamed x6, local copies, waits for them, and re-layouts  0.95 us
    pallas_call x1, Pallas kernels, on_device(): pl.pallas_call(near_kernel, out_shape=(windows, windows), in_specs=vmem(7...  0.94 us
    ppermute x4, waiting for transfers between devices, swap_rows(): lax.ppermute(cells, ('date', 'row'), [(date * rows_count + row, partner(d...  0.8 us
  transfers between devices with their start and end apart: 11, of which 5 were waited for; matrix products, arithmetic and copies ran while one was open for 0% of the time, Pallas kernels for 16%

commit v1 on v0

--- a/solution.py
+++ b/solution.py
@@ -191,7 +191,7 @@
 ):
     row_at, row_count = lax.axis_index("row"), lax.axis_size("row")
 
-    exists = (below & (row_at < row_count - 1)) | (jnp.logical_not(below) & (row_at > 0))
+    exists = exists_at(below)
 
     def mix_group(own_ref, other_ref, base, slot):
         group = base + slot
@@ -289,6 +289,17 @@
 def swapped(values):
     real = (lane_ids((1, LANES)) % 8) < 4
     return jnp.where(real, pltpu.roll(values, LANES - 4, axis=1), -pltpu.roll(values, 4, axis=1))
+
+
+def exists_at(below):
+    row_at, row_count = lax.axis_index("row"), lax.axis_size("row")
+    return (below & (row_at < row_count - 1)) | (jnp.logical_not(below) & (row_at > 0))
+
+
+def screen_kernel(near_ref, far_ref, near_out_ref, far_out_ref):
+    below = near_is_below()
+    near_out_ref[...] = jnp.where(exists_at(below), near_ref[...], 0.0)
+    far_out_ref[...] = jnp.where(exists_at(jnp.logical_not(below)), far_ref[...], 0.0)
 
 
 def near_kernel(
@@ -524,6 +535,16 @@
         cost_estimate=pl.CostEstimate(flops=4_000_000, bytes_accessed=1_000_000, transcendentals=0),
         name="prepare",
     )(offsets, masks)
+
+    near_a, far_a = pl.pallas_call(
+        screen_kernel,
+        out_shape=(half_shape, half_shape),
+        in_specs=vmem(2),
+        out_specs=tuple(vmem(2)),
+        compiler_params=small,
+        cost_estimate=moves,
+        name="screen",
+    )(near_a, far_a)
 
     half_scratch = [
         pltpu.VMEM((4, LANES, LANES), FLOAT),

time: 24.8 us -> 25.4 us (1.024)
  starting transfers between devices: 12.8 us -> 13.2 us
    ppermute x4, starting transfers between devices: 5.32 us -> 5.71 us  [swap_rows(): lax.ppermute(cells, ('date', 'row'), [(date * rows_count + row, partner(d...]
  transfers between devices with their start and end apart: 11 -> 11, of which waited for: 5 -> 4; matrix products, arithmetic and copies ran while one was open for 0% -> 0% of each run, Pallas kernels for 16% -> 16%
where the time goes in v1:
time: 25.4 us; the launch traced here: 25.2 us
  starting transfers between devices  13.2 us (52%)
  Pallas kernels  7.66 us (30%)
  waiting for transfers between devices  2.71 us (11%)
  local copies, waits for them, and re-layouts  0.96 us (4%)
  between operations  0.73 us (3%)
    ppermute x7, starting transfers between devices, on_device(): lax.ppermute(pieces[turn], 'date', [(i, i ^ turn) for i in range(GROUPS)])  7.46 us
    ppermute x4, starting transfers between devices, swap_rows(): lax.ppermute(cells, ('date', 'row'), [(date * rows_count + row, partner(d...  5.71 us
    pallas_call x1, Pallas kernels, on_device(): pl.pallas_call(link_kernel, out_shape=(jax.ShapeDtypeStruct((2 * NDATE *...  3.5 us
    pallas_call x1, Pallas kernels, on_device(): pl.pallas_call(prepare_kernel, out_shape=(jax.ShapeDtypeStruct((BLOCKS, 6...  2.92 us
    ppermute x7, waiting for transfers between devices, on_device(): lax.ppermute(pieces[turn], 'date', [(i, i ^ turn) for i in range(GROUPS)])  1.79 us
    unnamed x6, local copies, waits for them, and re-layouts  0.96 us
    pallas_call x1, Pallas kernels, on_device(): pl.pallas_call(near_kernel, out_shape=(windows, windows), in_specs=vmem(7...  0.94 us
    ppermute x4, waiting for transfers between devices, swap_rows(): lax.ppermute(cells, ('date', 'row'), [(date * rows_count + row, partner(d...  0.92 us
  transfers between devices with their start and end apart: 11, of which 4 were waited for; matrix products, arithmetic and copies ran while one was open for 0% of the time, Pallas kernels for 16%

profile of v1, /device:TPU:0, one launch (start us, length us, event | category | flops | bytes accessed | tf_op | source)
XLA Modules:
  0.0 25.2 jit_solution(8563939693091232239)
XLA Ops:
  0.6 0.0 copy-start
  0.6 0.9 %copy-done = f32[2,4,8,1024]{3,2,1,0:T(8,128)S(1)} copy-done((f32[2,4,8,1024]{3,2,1,0:T(8,128)S(1)}, f32[2,4,8,1024]{3,2,1,0:T(8,128)}, u32[]{:S(2)}) %copy-start) | copy-done | bytes 262168
  1.6 0.2 pack.1
  1.8 4.0 %collective-permute-start.3 = (f32[72,128]{1,0:T(8,128)S(1)}, f32[72,128]{1,0:T(8,128)S(1)}, u32[]{:S(2)}, u32[]{:S(2)}) collective-permute-start(f32[72,128]{1,0:T(8,128)S(1)} %get-tuple-element.25), channel_id=1, source_target_pairs={{0,24},{4,28},{8,16},{12,20},{16,8},{20,12},{24,0},{28,4},{1,25},{... | collective-permute-start | bytes 110600 | tf_op jit(solution)/shard_map/ppermute | solution.py:492
  5.7 0.0 collective-permute-start.4
  5.7 1.2 %collective-permute-start.5 = (f32[72,128]{1,0:T(8,128)S(1)}, f32[72,128]{1,0:T(8,128)S(1)}, u32[]{:S(2)}, u32[]{:S(2)}) collective-permute-start(f32[72,128]{1,0:T(8,128)S(1)} %get-tuple-element.27), channel_id=1, source_target_pairs={{0,16},{4,20},{8,24},{12,28},{16,0},{20,4},{24,8},{28,12},{1,17},{... | collective-permute-start | bytes 110600 | tf_op jit(solution)/shard_map/ppermute | solution.py:492
  6.9 0.6 %collective-permute-start.6 = (f32[72,128]{1,0:T(8,128)S(1)}, f32[72,128]{1,0:T(8,128)S(1)}, u32[]{:S(2)}, u32[]{:S(2)}) collective-permute-start(f32[72,128]{1,0:T(8,128)S(1)} %get-tuple-element.28), channel_id=1, source_target_pairs={{0,20},{4,16},{8,28},{12,24},{16,4},{20,0},{24,12},{28,8},{1,21},{... | collective-permute-start | bytes 110600 | tf_op jit(solution)/shard_map/ppermute | solution.py:492
  7.5 1.7 %collective-permute-start = (f32[72,128]{1,0:T(8,128)S(1)}, f32[72,128]{1,0:T(8,128)S(1)}, u32[]{:S(2)}, u32[]{:S(2)}) collective-permute-start(f32[72,128]{1,0:T(8,128)S(1)} %get-tuple-element.21), channel_id=1, source_target_pairs={{0,8},{4,12},{8,0},{12,4},{16,24},{20,28},{24,16},{28,20},{1,9},{5... | collective-permute-start | bytes 110600 | tf_op jit(solution)/shard_map/ppermute | solution.py:492
  9.2 0.0 collective-permute-done.3.rest_0_
  9.2 0.1 collective-permute-start.1
  9.2 1.0 %collective-permute-done.4.rest_1_ = f32[72,128]{1,0:T(8,128)S(1)} collective-permute-done((f32[72,128]{1,0:T(8,128)S(1)}, f32[72,128]{1,0:T(8,128)S(1)}, u32[]{:S(2)}, u32[]{:S(2)}) %collective-permute-start.4) | collective-permute-done | bytes 36896 | tf_op jit(solution)/shard_map/ppermute | solution.py:492
  10.3 0.0 collective-permute-start.2
  10.3 0.5 %collective-permute-done.5.rest_2_ = f32[72,128]{1,0:T(8,128)S(1)} collective-permute-done((f32[72,128]{1,0:T(8,128)S(1)}, f32[72,128]{1,0:T(8,128)S(1)}, u32[]{:S(2)}, u32[]{:S(2)}) %collective-permute-start.5) | collective-permute-done | bytes 36896 | tf_op jit(solution)/shard_map/ppermute | solution.py:492
  10.7 0.3 %collective-permute-done.6.rest_3_ = f32[72,128]{1,0:T(8,128)S(1)} collective-permute-done((f32[72,128]{1,0:T(8,128)S(1)}, f32[72,128]{1,0:T(8,128)S(1)}, u32[]{:S(2)}, u32[]{:S(2)}) %collective-permute-start.6) | collective-permute-done | bytes 36896 | tf_op jit(solution)/shard_map/ppermute | solution.py:492
  11.1 1.7 %collective-permute-start.8 = (f32[4,72,128]{2,1,0:T(8,128)S(1)}, f32[4,72,128]{2,1,0:T(8,128)S(1)}, u32[]{:S(2)}, u32[]{:S(2)}) collective-permute-start(f32[4,72,128]{2,1,0:T(8,128)S(1)} %join.3.own_a), channel_id=1, source_target_pairs={{0,1},{1,0},{2,3},{3,2},{4,12},{5,6},{6,5},{7,15},{8,9},{9,8},{10,... | collective-permute-start | bytes 442376 | tf_op jit(solution)/shard_map/ppermute | solution.py:470
  12.7 0.8 %collective-permute-start.9 = (f32[4,72,128]{2,1,0:T(8,128)S(1)}, f32[4,72,128]{2,1,0:T(8,128)S(1)}, u32[]{:S(2)}, u32[]{:S(2)}) collective-permute-start(f32[4,72,128]{2,1,0:T(8,128)S(1)} %join.3.own_a), channel_id=1, source_target_pairs={{0,8},{1,2},{2,1},{3,11},{4,5},{5,4},{6,7},{7,6},{8,0},{9,10},{10,... | collective-permute-start | bytes 442376 | tf_op jit(solution)/shard_map/ppermute | solution.py:470
  13.5 0.0 collective-permute-done.rest_0_
  13.5 0.0 collective-permute-done.1.rest_1_
  13.5 0.0 collective-permute-done.2.rest_2_
  13.6 0.0 copy-start.1
  13.6 0.0 copy-start.2
  13.6 2.4 %collective-permute-start.10 = (f32[4,72,128]{2,1,0:T(8,128)S(1)}, f32[4,72,128]{2,1,0:T(8,128)S(1)}, u32[]{:S(2)}, u32[]{:S(2)}) collective-permute-start(f32[4,72,128]{2,1,0:T(8,128)S(1)} %join.2.own_b), channel_id=1, source_target_pairs={{0,1},{1,0},{2,3},{3,2},{4,12},{5,6},{6,5},{7,15},{8,9},{9,8},{10,... | collective-permute-start | bytes 442376 | tf_op jit(solution)/shard_map/ppermute | solution.py:470
  16.0 0.8 %collective-permute-start.7 = (f32[4,72,128]{2,1,0:T(8,128)S(1)}, f32[4,72,128]{2,1,0:T(8,128)S(1)}, u32[]{:S(2)}, u32[]{:S(2)}) collective-permute-start(f32[4,72,128]{2,1,0:T(8,128)S(1)} %join.2.own_b), channel_id=1, source_target_pairs={{0,8},{1,2},{2,1},{3,11},{4,5},{5,4},{6,7},{7,6},{8,0},{9,10},{10,... | collective-permute-start | bytes 442376 | tf_op jit(solution)/shard_map/ppermute | solution.py:470
  16.8 0.0 copy-done.1
  16.8 2.9 %prepare.1 = (bf16[16,64,256]{2,1,0:T(8,128)(2,1)S(1)}, f32[8,128]{1,0:T(8,128)S(1)}, f32[8,64,128]{2,1,0:T(8,128)S(1)}, f32[8,8,128]{2,1,0:T(8,128)S(1)}, f32[8,8,128]{2,1,0:T(8,128)S(1)}) custom-call(s32[2,32]{1,0:T(2,128)S(1)} %copy-done.2, s32[5,8,128]{2,1,0:T(8,128)S(1)} %copy-done.1), custom_call_target="tpu_custom_call" | custom-call | flops 4000000 | bytes 1000000 | tf_op jit(solution)/shard_map/prepare/pallas_call | solution.py:522
  19.8 0.0 collective-permute-done.8.near_ref
  19.8 0.0 collective-permute-done.9.far_ref
  19.8 0.1 screen.1
  19.9 0.9 %collective-permute-done.10.near_b = f32[4,72,128]{2,1,0:T(8,128)S(1)} collective-permute-done((f32[4,72,128]{2,1,0:T(8,128)S(1)}, f32[4,72,128]{2,1,0:T(8,128)S(1)}, u32[]{:S(2)}, u32[]{:S(2)}) %collective-permute-start.10) | collective-permute-done | bytes 147488 | tf_op jit(solution)/shard_map/ppermute | solution.py:470
  20.8 0.9 %near.1 = (bf16[16,128,128]{2,1,0:T(8,128)(2,1)S(1)}, bf16[16,128,128]{2,1,0:T(8,128)(2,1)S(1)}) custom-call(f32[4,72,128]{2,1,0:T(8,128)S(1)} %join.2.own_b, f32[4,72,128]{2,1,0:T(8,128)S(1)} %join.3.own_a, f32[4,72,128]{2,1,0:T(8,128)S(1)} %collective-permute-done.10.near_b, f32[4,72,128]{2,1,0:T(8,128)S(1)} %get-tuple-element.33.near_a, ...), custom_call_target="tpu_custom_call" | custom-call | flops 200000000 | bytes 2000000 | tf_op jit(solution)/shard_map/near/pallas_call | solution.py:555
  21.7 0.0 collective-permute-done.7.far_b
  21.7 3.5 %link.1 = (f32[512,128]{1,0:T(8,128)}, f32[8,128]{1,0:T(8,128)}) custom-call(f32[4,72,128]{2,1,0:T(8,128)S(1)} %join.2.own_b, f32[4,72,128]{2,1,0:T(8,128)S(1)} %join.3.own_a, f32[4,72,128]{2,1,0:T(8,128)S(1)} %collective-permute-done.7.far_b, f32[4,72,128]{2,1,0:T(8,128)S(1)} %get-tuple-element.29.far_a, f32[8,64,128]{2,1,0:T(8,128)S(1)} %get-tuple-element.30.row_sub_ref, ...), custom_call_target="tpu_custom_call" | custom-call | flops 1000000000 | bytes 2000000 | tf_op jit(solution)/shard_map/link/pallas_call | solution.py:567
  (3 shorter events, 0.0 us)
Async XLA Ops:
  0.6 1.0 %copy-start = (f32[2,4,8,1024]{3,2,1,0:T(8,128)S(1)}, f32[2,4,8,1024]{3,2,1,0:T(8,128)}, u32[]{:S(2)}) copy-start(f32[2,4,8,1024]{3,2,1,0:T(8,128)} %param.3) | copy-start | bytes 786436
  1.8 7.4 %collective-permute-start.3 = (f32[72,128]{1,0:T(8,128)S(1)}, f32[72,128]{1,0:T(8,128)S(1)}, u32[]{:S(2)}, u32[]{:S(2)}) collective-permute-start(f32[72,128]{1,0:T(8,128)S(1)} %get-tuple-element.25), channel_id=1, source_target_pairs={{0,24},{4,28},{8,16},{12,20},{16,8},{20,12},{24,0},{28,4},{1,25},{... | collective-permute-start | bytes 110600 | tf_op jit(solution)/shard_map/ppermute | solution.py:492
  5.7 4.5 %collective-permute-start.4 = (f32[72,128]{1,0:T(8,128)S(1)}, f32[72,128]{1,0:T(8,128)S(1)}, u32[]{:S(2)}, u32[]{:S(2)}) collective-permute-start(f32[72,128]{1,0:T(8,128)S(1)} %get-tuple-element.26), channel_id=1, source_target_pairs={{0,28},{4,24},{8,20},{12,16},{16,12},{20,8},{24,4},{28,0},{1,29},{... | collective-permute-start | bytes 110600 | tf_op jit(solution)/shard_map/ppermute | solution.py:492
  5.7 5.0 %collective-permute-start.5 = (f32[72,128]{1,0:T(8,128)S(1)}, f32[72,128]{1,0:T(8,128)S(1)}, u32[]{:S(2)}, u32[]{:S(2)}) collective-permute-start(f32[72,128]{1,0:T(8,128)S(1)} %get-tuple-element.27), channel_id=1, source_target_pairs={{0,16},{4,20},{8,24},{12,28},{16,0},{20,4},{24,8},{28,12},{1,17},{... | collective-permute-start | bytes 110600 | tf_op jit(solution)/shard_map/ppermute | solution.py:492
  6.9 4.1 %collective-permute-start.6 = (f32[72,128]{1,0:T(8,128)S(1)}, f32[72,128]{1,0:T(8,128)S(1)}, u32[]{:S(2)}, u32[]{:S(2)}) collective-permute-start(f32[72,128]{1,0:T(8,128)S(1)} %get-tuple-element.28), channel_id=1, source_target_pairs={{0,20},{4,16},{8,28},{12,24},{16,4},{20,0},{24,12},{28,8},{1,21},{... | collective-permute-start | bytes 110600 | tf_op jit(solution)/shard_map/ppermute | solution.py:492
  7.5 6.1 %collective-permute-start = (f32[72,128]{1,0:T(8,128)S(1)}, f32[72,128]{1,0:T(8,128)S(1)}, u32[]{:S(2)}, u32[]{:S(2)}) collective-permute-start(f32[72,128]{1,0:T(8,128)S(1)} %get-tuple-element.21), channel_id=1, source_target_pairs={{0,8},{4,12},{8,0},{12,4},{16,24},{20,28},{24,16},{28,20},{1,9},{5... | collective-permute-start | bytes 110600 | tf_op jit(solution)/shard_map/ppermute | solution.py:492
  9.2 4.4 %collective-permute-start.1 = (f32[72,128]{1,0:T(8,128)S(1)}, f32[72,128]{1,0:T(8,128)S(1)}, u32[]{:S(2)}, u32[]{:S(2)}) collective-permute-start(f32[72,128]{1,0:T(8,128)S(1)} %get-tuple-element.22), channel_id=1, source_target_pairs={{0,12},{4,8},{8,4},{12,0},{16,28},{20,24},{24,20},{28,16},{1,13},{... | collective-permute-start | bytes 110600 | tf_op jit(solution)/shard_map/ppermute | solution.py:492
  10.3 3.3 %collective-permute-start.2 = (f32[72,128]{1,0:T(8,128)S(1)}, f32[72,128]{1,0:T(8,128)S(1)}, u32[]{:S(2)}, u32[]{:S(2)}) collective-permute-start(f32[72,128]{1,0:T(8,128)S(1)} %get-tuple-element.23), channel_id=1, source_target_pairs={{0,4},{4,0},{8,12},{12,8},{16,20},{20,16},{24,28},{28,24},{1,5},{5... | collective-permute-start | bytes 110600 | tf_op jit(solution)/shard_map/ppermute | solution.py:492
  11.1 8.7 %collective-permute-start.8 = (f32[4,72,128]{2,1,0:T(8,128)S(1)}, f32[4,72,128]{2,1,0:T(8,128)S(1)}, u32[]{:S(2)}, u32[]{:S(2)}) collective-permute-start(f32[4,72,128]{2,1,0:T(8,128)S(1)} %join.3.own_a), channel_id=1, source_target_pairs={{0,1},{1,0},{2,3},{3,2},{4,12},{5,6},{6,5},{7,15},{8,9},{9,8},{10,... | collective-permute-start | bytes 442376 | tf_op jit(solution)/shard_map/ppermute | solution.py:470
  12.7 7.1 %collective-permute-start.9 = (f32[4,72,128]{2,1,0:T(8,128)S(1)}, f32[4,72,128]{2,1,0:T(8,128)S(1)}, u32[]{:S(2)}, u32[]{:S(2)}) collective-permute-start(f32[4,72,128]{2,1,0:T(8,128)S(1)} %join.3.own_a), channel_id=1, source_target_pairs={{0,8},{1,2},{2,1},{3,11},{4,5},{5,4},{6,7},{7,6},{8,0},{9,10},{10,... | collective-permute-start | bytes 442376 | tf_op jit(solution)/shard_map/ppermute | solution.py:470
  13.6 3.3 %copy-start.1 = (s32[5,8,128]{2,1,0:T(8,128)S(1)}, s32[5,8,128]{2,1,0:T(8,128)}, u32[]{:S(2)}) copy-start(s32[5,8,128]{2,1,0:T(8,128)} %masks_ref.1) | copy-start | bytes 61444
  13.6 3.3 %copy-start.2 = (s32[2,32]{1,0:T(2,128)S(1)}, s32[2,32]{1,0:T(2,128)}, u32[]{:S(2)}) copy-start(s32[2,32]{1,0:T(2,128)} %offsets_ref.1) | copy-start | bytes 772
  13.6 7.2 %collective-permute-start.10 = (f32[4,72,128]{2,1,0:T(8,128)S(1)}, f32[4,72,128]{2,1,0:T(8,128)S(1)}, u32[]{:S(2)}, u32[]{:S(2)}) collective-permute-start(f32[4,72,128]{2,1,0:T(8,128)S(1)} %join.2.own_b), channel_id=1, source_target_pairs={{0,1},{1,0},{2,3},{3,2},{4,12},{5,6},{6,5},{7,15},{8,9},{9,8},{10,... | collective-permute-start | bytes 442376 | tf_op jit(solution)/shard_map/ppermute | solution.py:470
  16.0 5.7 %collective-permute-start.7 = (f32[4,72,128]{2,1,0:T(8,128)S(1)}, f32[4,72,128]{2,1,0:T(8,128)S(1)}, u32[]{:S(2)}, u32[]{:S(2)}) collective-permute-start(f32[4,72,128]{2,1,0:T(8,128)S(1)} %join.2.own_b), channel_id=1, source_target_pairs={{0,8},{1,2},{2,1},{3,11},{4,5},{5,4},{6,7},{7,6},{8,0},{9,10},{10,... | collective-permute-start | bytes 442376 | tf_op jit(solution)/shard_map/ppermute | solution.py:470

commit v2 on v0

--- a/solution.py
+++ b/solution.py
@@ -178,22 +178,15 @@
     return (lax.axis_index("row") + lax.axis_index("date")) % 2 == 0
 
 
-def resample_rows(
-    base,
-    own_refs,
-    other_refs,
-    below,
-    row_sub_ref,
-    row_lane_ref,
-    mixed_ref,
-    rims_ref,
-    turned_ref,
-):
+def exists_at(below):
     row_at, row_count = lax.axis_index("row"), lax.axis_size("row")
-
-    exists = (below & (row_at < row_count - 1)) | (jnp.logical_not(below) & (row_at > 0))
-
-    def mix_group(own_ref, other_ref, base, slot):
+    return (below & (row_at < row_count - 1)) | (jnp.logical_not(below) & (row_at > 0))
+
+
+def mix_rows(base, own_ref, other_ref, below, row_sub_ref, mixed_ref):
+    exists = exists_at(below)
+
+    def mix_group(slot, carry):
         group = base + slot
         weights = [
             row_sub_ref[tap, pl.ds(pl.multiple_of(group * TILE, TILE), TILE), :]
@@ -212,13 +205,13 @@
                 mixed = mixed + weights[tap] * raw[row + 1 + tap]
             start = pl.multiple_of((row // 4) * 64 + group * TILE, TILE)
             mixed_ref[row % 4, pl.ds(start, TILE), :] = mixed
-
-    def mix_slot(slot, carry):
-        mix_group(own_refs[0], other_refs[0], base, slot)
-        mix_group(own_refs[1], other_refs[1], 4 - base, slot)
         return carry
 
-    lax.fori_loop(0, GROUPS // 2, mix_slot, 0)
+    lax.fori_loop(0, GROUPS // 2, mix_group, 0, unroll=2)
+
+
+def turn_rows(base, own_refs, other_refs, below, row_lane_ref, mixed_ref, rims_ref, turned_ref):
+    exists = exists_at(below)
 
     lanes = lane_ids((1, LANES))
     lower = lanes < 64
@@ -296,28 +289,27 @@
     own_a,
     near_b,
     near_a,
+    picks_ref,
     row_sub_ref,
     row_lane_ref,
     col_lane_ref,
     z_ref,
     y_ref,
+    first_ref,
     mixed_ref,
     rims_ref,
     turned_ref,
 ):
     below = near_is_below()
-    resample_rows(
-        first_group(),
-        (own_a, own_b),
-        (near_a, near_b),
-        below,
-        row_sub_ref,
-        row_lane_ref,
-        mixed_ref,
-        rims_ref,
-        turned_ref,
+    base = first_group()
+    mix_rows(base, own_a, near_a, below, row_sub_ref, mixed_ref)
+    mix_rows(4 - base, own_b, near_b, below, row_sub_ref, mixed_ref)
+    turn_rows(
+        base, (own_a, own_b), (near_a, near_b), below, row_lane_ref, mixed_ref, rims_ref, turned_ref
     )
     resample_columns(below, col_lane_ref, z_ref, y_ref, turned_ref, 0, BLOCKS)
+    for block in range(BLOCKS):
+        first_ref[block] = dot(picks_ref[block, :, :LANES], y_ref[block], (1, 0))
 
 
 def link_kernel(
@@ -329,7 +321,7 @@
     row_lane_ref,
     col_lane_ref,
     near_z_ref,
-    near_y_ref,
+    near_first_ref,
     picks_ref,
     population_ref,
     linked_ref,
@@ -345,16 +337,11 @@
     chosen_ref,
 ):
     below = jnp.logical_not(near_is_below())
-    resample_rows(
-        first_group(),
-        (own_a, own_b),
-        (far_a, far_b),
-        below,
-        row_sub_ref,
-        row_lane_ref,
-        mixed_ref,
-        rims_ref,
-        turned_ref,
+    base = first_group()
+    mix_rows(base, own_a, far_a, below, row_sub_ref, mixed_ref)
+    mix_rows(4 - base, own_b, far_b, below, row_sub_ref, mixed_ref)
+    turn_rows(
+        base, (own_a, own_b), (far_a, far_b), below, row_lane_ref, mixed_ref, rims_ref, turned_ref
     )
     lower = lane_ids((1, LANES)) < 64
 
@@ -363,8 +350,8 @@
 
     def first_phase(first, count):
         for block in range(first, first + count):
-            y = jnp.concatenate([near_y_ref[block], far_y_ref[block]], axis=0)
-            vector = dot(picks_ref[block], y, (1, 0))
+            vector = dot(picks_ref[block, :, LANES:], far_y_ref[block], (1, 0))
+            vector = vector + near_first_ref[block]
             vector = vector + pltpu.roll(vector, 64, axis=1)
             high, low = split_halves(jnp.concatenate([vector, swapped(vector)], axis=0))
             first_ref[block] = vector
@@ -531,18 +518,22 @@
         pltpu.VMEM((4, LANES + 16, LANES), FLOAT),
     ]
     windows = jax.ShapeDtypeStruct((BLOCKS, LANES, LANES), HALF_FLOAT)
-    near_z, near_y = pl.pallas_call(
+    near_z, _, near_first = pl.pallas_call(
         near_kernel,
-        out_shape=(windows, windows),
-        in_specs=vmem(7),
-        out_specs=tuple(vmem(2)),
+        out_shape=(
+            windows,
+            windows,
+            jax.ShapeDtypeStruct((BLOCKS, 64, LANES), FLOAT),
+        ),
+        in_specs=vmem(8),
+        out_specs=tuple(vmem(3)),
         scratch_shapes=half_scratch,
         compiler_params=small,
         cost_estimate=pl.CostEstimate(
             flops=200_000_000, bytes_accessed=2_000_000, transcendentals=0
         ),
         name="near",
-    )(*own[::-1], near_b, near_a, row_sub, row_lane, col_lane)
+    )(*own[::-1], near_b, near_a, picks, row_sub, row_lane, col_lane)
     linked, eigen = pl.pallas_call(
         link_kernel,
         out_shape=(
@@ -567,7 +558,7 @@
             flops=1_000_000_000, bytes_accessed=2_000_000, transcendentals=0
         ),
         name="link",
-    )(*own[::-1], far_b, far_a, row_sub, row_lane, col_lane, near_z, near_y, picks, population)
+    )(*own[::-1], far_b, far_a, row_sub, row_lane, col_lane, near_z, near_first, picks, population)
     return linked.reshape(2, NDATE, TILE, LANES), eigen
 
 

time: 24.8 us -> 24.9 us (level)
  Pallas kernels: 7.6 us -> 8.36 us
  waiting for transfers between devices: 2.63 us -> 1.94 us
    pallas_call x1, Pallas kernels: 0.94 us -> 1.73 us  [on_device(): pl.pallas_call(near_kernel, out_shape=(windows, windows, jax.ShapeDtypeSt...]
    ppermute x4, waiting for transfers between devices: 0.8 us -> 0.11 us  [swap_rows(): lax.ppermute(cells, ('date', 'row'), [(date * rows_count + row, partner(d...]
  transfers between devices with their start and end apart: 11 -> 11, of which waited for: 5 -> 4; matrix products, arithmetic and copies ran while one was open for 0% -> 0% of each run, Pallas kernels for 16% -> 19%
where the time goes in v2:
time: 24.9 us; the launch traced here: 24.7 us
  starting transfers between devices  12.8 us (51%)
  Pallas kernels  8.36 us (34%)
  waiting for transfers between devices  1.94 us (8%)
  local copies, waits for them, and re-layouts  0.95 us (4%)
  between operations  0.69 us (3%)
    ppermute x7, starting transfers between devices, on_device(): lax.ppermute(pieces[turn], 'date', [(i, i ^ turn) for i in range(GROUPS)])  7.46 us
    ppermute x4, starting transfers between devices, swap_rows(): lax.ppermute(cells, ('date', 'row'), [(date * rows_count + row, partner(d...  5.32 us
    pallas_call x1, Pallas kernels, on_device(): pl.pallas_call(link_kernel, out_shape=(jax.ShapeDtypeStruct((2 * NDATE *...  3.47 us
    pallas_call x1, Pallas kernels, on_device(): pl.pallas_call(prepare_kernel, out_shape=(jax.ShapeDtypeStruct((BLOCKS, 6...  2.92 us
    ppermute x7, waiting for transfers between devices, on_device(): lax.ppermute(pieces[turn], 'date', [(i, i ^ turn) for i in range(GROUPS)])  1.83 us
    pallas_call x1, Pallas kernels, on_device(): pl.pallas_call(near_kernel, out_shape=(windows, windows, jax.ShapeDtypeSt...  1.73 us
    unnamed x6, local copies, waits for them, and re-layouts  0.95 us
  transfers between devices with their start and end apart: 11, of which 4 were waited for; matrix products, arithmetic and copies ran while one was open for 0% of the time, Pallas kernels for 19%

profile of v2, /device:TPU:0, one launch (start us, length us, event | category | flops | bytes accessed | tf_op | source)
XLA Modules:
  0.0 24.7 jit_solution(12771724819318721782)
XLA Ops:
  0.6 0.0 copy-start
  0.6 0.9 %copy-done = f32[2,4,8,1024]{3,2,1,0:T(8,128)S(1)} copy-done((f32[2,4,8,1024]{3,2,1,0:T(8,128)S(1)}, f32[2,4,8,1024]{3,2,1,0:T(8,128)}, u32[]{:S(2)}) %copy-start) | copy-done | bytes 262168
  1.6 0.2 pack.1
  1.8 4.0 %collective-permute-start.3 = (f32[72,128]{1,0:T(8,128)S(1)}, f32[72,128]{1,0:T(8,128)S(1)}, u32[]{:S(2)}, u32[]{:S(2)}) collective-permute-start(f32[72,128]{1,0:T(8,128)S(1)} %get-tuple-element.23), channel_id=1, source_target_pairs={{0,24},{4,28},{8,16},{12,20},{16,8},{20,12},{24,0},{28,4},{1,25},{... | collective-permute-start | bytes 110600 | tf_op jit(solution)/shard_map/ppermute | solution.py:468
  5.7 0.0 collective-permute-start.4
  5.7 1.2 %collective-permute-start.5 = (f32[72,128]{1,0:T(8,128)S(1)}, f32[72,128]{1,0:T(8,128)S(1)}, u32[]{:S(2)}, u32[]{:S(2)}) collective-permute-start(f32[72,128]{1,0:T(8,128)S(1)} %get-tuple-element.25), channel_id=1, source_target_pairs={{0,16},{4,20},{8,24},{12,28},{16,0},{20,4},{24,8},{28,12},{1,17},{... | collective-permute-start | bytes 110600 | tf_op jit(solution)/shard_map/ppermute | solution.py:468
  6.9 0.6 %collective-permute-start.6 = (f32[72,128]{1,0:T(8,128)S(1)}, f32[72,128]{1,0:T(8,128)S(1)}, u32[]{:S(2)}, u32[]{:S(2)}) collective-permute-start(f32[72,128]{1,0:T(8,128)S(1)} %get-tuple-element.26), channel_id=1, source_target_pairs={{0,20},{4,16},{8,28},{12,24},{16,4},{20,0},{24,12},{28,8},{1,21},{... | collective-permute-start | bytes 110600 | tf_op jit(solution)/shard_map/ppermute | solution.py:468
  7.5 1.7 %collective-permute-start = (f32[72,128]{1,0:T(8,128)S(1)}, f32[72,128]{1,0:T(8,128)S(1)}, u32[]{:S(2)}, u32[]{:S(2)}) collective-permute-start(f32[72,128]{1,0:T(8,128)S(1)} %get-tuple-element.19), channel_id=1, source_target_pairs={{0,8},{4,12},{8,0},{12,4},{16,24},{20,28},{24,16},{28,20},{1,9},{5... | collective-permute-start | bytes 110600 | tf_op jit(solution)/shard_map/ppermute | solution.py:468
  9.2 0.0 collective-permute-done.3.rest_0_
  9.2 0.1 collective-permute-start.1
  9.2 1.0 %collective-permute-done.4.rest_1_ = f32[72,128]{1,0:T(8,128)S(1)} collective-permute-done((f32[72,128]{1,0:T(8,128)S(1)}, f32[72,128]{1,0:T(8,128)S(1)}, u32[]{:S(2)}, u32[]{:S(2)}) %collective-permute-start.4) | collective-permute-done | bytes 36896 | tf_op jit(solution)/shard_map/ppermute | solution.py:468
  10.3 0.0 collective-permute-start.2
  10.3 0.5 %collective-permute-done.5.rest_2_ = f32[72,128]{1,0:T(8,128)S(1)} collective-permute-done((f32[72,128]{1,0:T(8,128)S(1)}, f32[72,128]{1,0:T(8,128)S(1)}, u32[]{:S(2)}, u32[]{:S(2)}) %collective-permute-start.5) | collective-permute-done | bytes 36896 | tf_op jit(solution)/shard_map/ppermute | solution.py:468
  10.7 0.3 %collective-permute-done.6.rest_3_ = f32[72,128]{1,0:T(8,128)S(1)} collective-permute-done((f32[72,128]{1,0:T(8,128)S(1)}, f32[72,128]{1,0:T(8,128)S(1)}, u32[]{:S(2)}, u32[]{:S(2)}) %collective-permute-start.6) | collective-permute-done | bytes 36896 | tf_op jit(solution)/shard_map/ppermute | solution.py:468
  11.1 1.7 %collective-permute-start.10 = (f32[4,72,128]{2,1,0:T(8,128)S(1)}, f32[4,72,128]{2,1,0:T(8,128)S(1)}, u32[]{:S(2)}, u32[]{:S(2)}) collective-permute-start(f32[4,72,128]{2,1,0:T(8,128)S(1)} %join.3.own_a), channel_id=1, source_target_pairs={{0,1},{1,0},{2,3},{3,2},{4,12},{5,6},{6,5},{7,15},{8,9},{9,8},{10,... | collective-permute-start | bytes 442376 | tf_op jit(solution)/shard_map/ppermute | solution.py:446
  12.7 0.0 collective-permute-done.rest_0_
  12.7 0.0 collective-permute-done.1.rest_1_
  12.8 0.0 collective-permute-done.2.rest_2_
  12.8 0.0 copy-start.1
  12.8 0.0 copy-start.2
  12.8 1.6 %collective-permute-start.9 = (f32[4,72,128]{2,1,0:T(8,128)S(1)}, f32[4,72,128]{2,1,0:T(8,128)S(1)}, u32[]{:S(2)}, u32[]{:S(2)}) collective-permute-start(f32[4,72,128]{2,1,0:T(8,128)S(1)} %join.2.own_b), channel_id=1, source_target_pairs={{0,1},{1,0},{2,3},{3,2},{4,12},{5,6},{6,5},{7,15},{8,9},{9,8},{10,... | collective-permute-start | bytes 442376 | tf_op jit(solution)/shard_map/ppermute | solution.py:446
  14.4 0.8 %collective-permute-start.8 = (f32[4,72,128]{2,1,0:T(8,128)S(1)}, f32[4,72,128]{2,1,0:T(8,128)S(1)}, u32[]{:S(2)}, u32[]{:S(2)}) collective-permute-start(f32[4,72,128]{2,1,0:T(8,128)S(1)} %join.3.own_a), channel_id=1, source_target_pairs={{0,8},{1,2},{2,1},{3,11},{4,5},{5,4},{6,7},{7,6},{8,0},{9,10},{10,... | collective-permute-start | bytes 442376 | tf_op jit(solution)/shard_map/ppermute | solution.py:446
  15.2 1.3 %collective-permute-start.7 = (f32[4,72,128]{2,1,0:T(8,128)S(1)}, f32[4,72,128]{2,1,0:T(8,128)S(1)}, u32[]{:S(2)}, u32[]{:S(2)}) collective-permute-start(f32[4,72,128]{2,1,0:T(8,128)S(1)} %join.2.own_b), channel_id=1, source_target_pairs={{0,8},{1,2},{2,1},{3,11},{4,5},{5,4},{6,7},{7,6},{8,0},{9,10},{10,... | collective-permute-start | bytes 442376 | tf_op jit(solution)/shard_map/ppermute | solution.py:446
  16.5 0.0 copy-done.1
  16.5 0.0 copy-done.2
  16.5 2.9 %prepare.1 = (bf16[16,64,256]{2,1,0:T(8,128)(2,1)S(1)}, f32[8,128]{1,0:T(8,128)S(1)}, f32[8,64,128]{2,1,0:T(8,128)S(1)}, f32[8,8,128]{2,1,0:T(8,128)S(1)}, f32[8,8,128]{2,1,0:T(8,128)S(1)}) custom-call(s32[2,32]{1,0:T(2,128)S(1)} %copy-done.2, s32[5,8,128]{2,1,0:T(8,128)S(1)} %copy-done.1), custom_call_target="tpu_custom_call" | custom-call | flops 4000000 | bytes 1000000 | tf_op jit(solution)/shard_map/prepare/pallas_call | solution.py:498
  19.4 0.0 collective-permute-done.10.near_a
  19.4 0.1 collective-permute-done.9.near_b
  19.5 1.7 %near.1 = (bf16[16,128,128]{2,1,0:T(8,128)(2,1)S(1)}, bf16[16,128,128]{2,1,0:T(8,128)(2,1)}, f32[16,64,128]{2,1,0:T(8,128)S(1)}) custom-call(f32[4,72,128]{2,1,0:T(8,128)S(1)} %join.2.own_b, f32[4,72,128]{2,1,0:T(8,128)S(1)} %join.3.own_a, f32[4,72,128]{2,1,0:T(8,128)S(1)} %collective-permute-done.9.near_b, ...), custom_call_target="tpu_custom_call" | custom-call | flops 200000000 | bytes 2000000 | tf_op jit(solution)/shard_map/near/pallas_call | solution.py:521
  21.2 0.0 collective-permute-done.8.far_a
  21.2 0.0 collective-permute-done.7.far_b
  21.2 3.5 %link.1 = (f32[512,128]{1,0:T(8,128)}, f32[8,128]{1,0:T(8,128)}) custom-call(f32[4,72,128]{2,1,0:T(8,128)S(1)} %join.2.own_b, f32[4,72,128]{2,1,0:T(8,128)S(1)} %join.3.own_a, f32[4,72,128]{2,1,0:T(8,128)S(1)} %collective-permute-done.7.far_b, f32[4,72,128]{2,1,0:T(8,128)S(1)} %collective-permute-done.8.far_a, ...), custom_call_target="tpu_custom_call" | custom-call | flops 1000000000 | bytes 2000000 | tf_op jit(solution)/shard_map/link/pallas_call | solution.py:537
  (2 shorter events, 0.0 us)
Async XLA Ops:
  0.6 1.0 %copy-start = (f32[2,4,8,1024]{3,2,1,0:T(8,128)S(1)}, f32[2,4,8,1024]{3,2,1,0:T(8,128)}, u32[]{:S(2)}) copy-start(f32[2,4,8,1024]{3,2,1,0:T(8,128)} %param.3) | copy-start | bytes 786436
  1.8 7.4 %collective-permute-start.3 = (f32[72,128]{1,0:T(8,128)S(1)}, f32[72,128]{1,0:T(8,128)S(1)}, u32[]{:S(2)}, u32[]{:S(2)}) collective-permute-start(f32[72,128]{1,0:T(8,128)S(1)} %get-tuple-element.23), channel_id=1, source_target_pairs={{0,24},{4,28},{8,16},{12,20},{16,8},{20,12},{24,0},{28,4},{1,25},{... | collective-permute-start | bytes 110600 | tf_op jit(solution)/shard_map/ppermute | solution.py:468
  5.7 4.5 %collective-permute-start.4 = (f32[72,128]{1,0:T(8,128)S(1)}, f32[72,128]{1,0:T(8,128)S(1)}, u32[]{:S(2)}, u32[]{:S(2)}) collective-permute-start(f32[72,128]{1,0:T(8,128)S(1)} %get-tuple-element.24), channel_id=1, source_target_pairs={{0,28},{4,24},{8,20},{12,16},{16,12},{20,8},{24,4},{28,0},{1,29},{... | collective-permute-start | bytes 110600 | tf_op jit(solution)/shard_map/ppermute | solution.py:468
  5.7 5.0 %collective-permute-start.5 = (f32[72,128]{1,0:T(8,128)S(1)}, f32[72,128]{1,0:T(8,128)S(1)}, u32[]{:S(2)}, u32[]{:S(2)}) collective-permute-start(f32[72,128]{1,0:T(8,128)S(1)} %get-tuple-element.25), channel_id=1, source_target_pairs={{0,16},{4,20},{8,24},{12,28},{16,0},{20,4},{24,8},{28,12},{1,17},{... | collective-permute-start | bytes 110600 | tf_op jit(solution)/shard_map/ppermute | solution.py:468
  6.9 4.1 %collective-permute-start.6 = (f32[72,128]{1,0:T(8,128)S(1)}, f32[72,128]{1,0:T(8,128)S(1)}, u32[]{:S(2)}, u32[]{:S(2)}) collective-permute-start(f32[72,128]{1,0:T(8,128)S(1)} %get-tuple-element.26), channel_id=1, source_target_pairs={{0,20},{4,16},{8,28},{12,24},{16,4},{20,0},{24,12},{28,8},{1,21},{... | collective-permute-start | bytes 110600 | tf_op jit(solution)/shard_map/ppermute | solution.py:468
  7.5 5.2 %collective-permute-start = (f32[72,128]{1,0:T(8,128)S(1)}, f32[72,128]{1,0:T(8,128)S(1)}, u32[]{:S(2)}, u32[]{:S(2)}) collective-permute-start(f32[72,128]{1,0:T(8,128)S(1)} %get-tuple-element.19), channel_id=1, source_target_pairs={{0,8},{4,12},{8,0},{12,4},{16,24},{20,28},{24,16},{28,20},{1,9},{5... | collective-permute-start | bytes 110600 | tf_op jit(solution)/shard_map/ppermute | solution.py:468
  9.2 3.6 %collective-permute-start.1 = (f32[72,128]{1,0:T(8,128)S(1)}, f32[72,128]{1,0:T(8,128)S(1)}, u32[]{:S(2)}, u32[]{:S(2)}) collective-permute-start(f32[72,128]{1,0:T(8,128)S(1)} %get-tuple-element.20), channel_id=1, source_target_pairs={{0,12},{4,8},{8,4},{12,0},{16,28},{20,24},{24,20},{28,16},{1,13},{... | collective-permute-start | bytes 110600 | tf_op jit(solution)/shard_map/ppermute | solution.py:468
  10.3 2.5 %collective-permute-start.2 = (f32[72,128]{1,0:T(8,128)S(1)}, f32[72,128]{1,0:T(8,128)S(1)}, u32[]{:S(2)}, u32[]{:S(2)}) collective-permute-start(f32[72,128]{1,0:T(8,128)S(1)} %get-tuple-element.21), channel_id=1, source_target_pairs={{0,4},{4,0},{8,12},{12,8},{16,20},{20,16},{24,28},{28,24},{1,5},{5... | collective-permute-start | bytes 110600 | tf_op jit(solution)/shard_map/ppermute | solution.py:468
  11.1 8.3 %collective-permute-start.10 = (f32[4,72,128]{2,1,0:T(8,128)S(1)}, f32[4,72,128]{2,1,0:T(8,128)S(1)}, u32[]{:S(2)}, u32[]{:S(2)}) collective-permute-start(f32[4,72,128]{2,1,0:T(8,128)S(1)} %join.3.own_a), channel_id=1, source_target_pairs={{0,1},{1,0},{2,3},{3,2},{4,12},{5,6},{6,5},{7,15},{8,9},{9,8},{10,... | collective-permute-start | bytes 442376 | tf_op jit(solution)/shard_map/ppermute | solution.py:446
  12.8 3.7 %copy-start.1 = (s32[5,8,128]{2,1,0:T(8,128)S(1)}, s32[5,8,128]{2,1,0:T(8,128)}, u32[]{:S(2)}) copy-start(s32[5,8,128]{2,1,0:T(8,128)} %masks_ref.1) | copy-start | bytes 61444
  12.8 3.7 %copy-start.2 = (s32[2,32]{1,0:T(2,128)S(1)}, s32[2,32]{1,0:T(2,128)}, u32[]{:S(2)}) copy-start(s32[2,32]{1,0:T(2,128)} %offsets_ref.1) | copy-start | bytes 772
  12.8 6.7 %collective-permute-start.9 = (f32[4,72,128]{2,1,0:T(8,128)S(1)}, f32[4,72,128]{2,1,0:T(8,128)S(1)}, u32[]{:S(2)}, u32[]{:S(2)}) collective-permute-start(f32[4,72,128]{2,1,0:T(8,128)S(1)} %join.2.own_b), channel_id=1, source_target_pairs={{0,1},{1,0},{2,3},{3,2},{4,12},{5,6},{6,5},{7,15},{8,9},{9,8},{10,... | collective-permute-start | bytes 442376 | tf_op jit(solution)/shard_map/ppermute | solution.py:446
  14.4 6.8 %collective-permute-start.8 = (f32[4,72,128]{2,1,0:T(8,128)S(1)}, f32[4,72,128]{2,1,0:T(8,128)S(1)}, u32[]{:S(2)}, u32[]{:S(2)}) collective-permute-start(f32[4,72,128]{2,1,0:T(8,128)S(1)} %join.3.own_a), channel_id=1, source_target_pairs={{0,8},{1,2},{2,1},{3,11},{4,5},{5,4},{6,7},{7,6},{8,0},{9,10},{10,... | collective-permute-start | bytes 442376 | tf_op jit(solution)/shard_map/ppermute | solution.py:446
  15.2 6.0 %collective-permute-start.7 = (f32[4,72,128]{2,1,0:T(8,128)S(1)}, f32[4,72,128]{2,1,0:T(8,128)S(1)}, u32[]{:S(2)}, u32[]{:S(2)}) collective-permute-start(f32[4,72,128]{2,1,0:T(8,128)S(1)} %join.2.own_b), channel_id=1, source_target_pairs={{0,8},{1,2},{2,1},{3,11},{4,5},{5,4},{6,7},{7,6},{8,0},{9,10},{10,... | collective-permute-start | bytes 442376 | tf_op jit(solution)/shard_map/ppermute | solution.py:446
